TPU v7x, 32 devices: a whole 2x2x4 slice. The times are simulated.
32 devices in a mesh: req: 16 (over z, y, x), tp: 2 (over core).
Axes of the slice: x: 2, y: 2, z: 4, core: 2. Of those that a mesh axis runs over, the one named last changes fastest.
Arguments:
- residual: bfloat16 [512, 2048], P('req'), may hold values from -6 to 6
- fresh_qkv: bfloat16 [512, 3, 2048], P('req', None, 'tp'), may hold values from -32 to 32
- kv_cache: bfloat16 [512, 24, 2, 2048], P('req', None, None, 'tp'), may hold values from -32 to 32
- cache_len: int32 [512], P('req'), may hold values from 2 to 24, as said below
- out_proj: bfloat16 [2048, 2048], P('tp'), may hold values from -0.125 to 0.125
- norm_gain: float32 [2048], replicated, may hold values from 0.1 to 1.9
- router_weight: float32 [2048, 16], replicated, may hold values from -7.9549513 to 7.9549513
- expert_ids: int32 [512, 8], P('req'), may hold values from 0 to 15, all different within a row; in each aligned block of 32 rows (0 to 31, 32 to 63, ...) at most 32 rows name the same one
- gate_up: bfloat16 [16, 2048, 2, 1024], P('req', None, None, 'tp'), may hold values from -0.125 to 0.125
- down_proj: bfloat16 [16, 1024, 2048], P('req', 'tp'), may hold values from -0.1875 to 0.1875
Outputs:
- layer_out: bfloat16 [512, 2048], P('req', 'tp')
Inputs may be any that keep to these rules, and one draw needn't show every extreme that they name: `expert_ids`: each row names 8 different experts; among the 32 rows of one device no expert is named by more than 32 rows, and some device reaches 32. `cache_len`: some request uses all 24 positions.
All inputs are finite; a program needn't handle non-finite values.
Results may differ from a plain program's by a relative error of at most 0.018.
Values may be sent and summed in bfloat16 or wider, within the bound.
A program may use at most 128 MiB of HBM per device.

v0:
```python
import jax
import jax.numpy as jnp
from jax import lax
from jax.sharding import PartitionSpec as P

HD = 128


def rms_normed(hidden_in, gain):
    values = hidden_in.astype(jnp.float32)
    scale_inv = lax.rsqrt(jnp.mean(values * values, axis=-1, keepdims=True) + 1e-05)
    return (values * scale_inv * gain).astype(jnp.bfloat16)


def attend(fresh_qkv, kv_cache, cache_len):
    requests, ctx_len = (kv_cache.shape[0], kv_cache.shape[1])
    local_heads = fresh_qkv.shape[2] // HD
    queries = fresh_qkv[:, 0].reshape(requests, local_heads, HD)
    new_keys = fresh_qkv[:, 1].reshape(requests, local_heads, HD)
    new_values = fresh_qkv[:, 2].reshape(requests, local_heads, HD)
    cache_keys = kv_cache[:, :, 0].reshape(requests, ctx_len, local_heads, HD)
    cache_values = kv_cache[:, :, 1].reshape(requests, ctx_len, local_heads, HD)
    factor = HD ** (-0.5)
    scores = (
        jnp.einsum("nhd,nchd->nhc", queries, cache_keys, preferred_element_type=jnp.float32)
        * factor
    )
    own_score = (
        jnp.einsum("nhd,nhd->nh", queries, new_keys, preferred_element_type=jnp.float32) * factor
    )
    valid = (jnp.arange(ctx_len, dtype=jnp.int32)[None, :] < cache_len[:, None])[:, None, :]
    masked = jnp.where(valid, scores, -jnp.inf)
    top_score = jnp.maximum(jnp.max(masked, axis=-1), own_score)
    expos = jnp.where(valid, jnp.exp(masked - top_score[..., None]), 0.0)
    own_expo = jnp.exp(own_score - top_score)
    total = jnp.sum(expos, axis=-1) + own_expo
    weights = (expos / total[..., None]).astype(jnp.bfloat16)
    own_weight = (own_expo / total).astype(jnp.bfloat16)
    mixed = jnp.einsum("nhc,nchd->nhd", weights, cache_values, preferred_element_type=jnp.float32)
    mixed = mixed + own_weight.astype(jnp.float32)[..., None] * new_values.astype(jnp.float32)
    return mixed.astype(jnp.bfloat16).reshape(requests, local_heads * HD)


def local(
    residual,
    fresh_qkv,
    kv_cache,
    cache_len,
    out_proj,
    norm_gain,
    router_weight,
    expert_ids,
    gate_up,
    down_proj,
):
    tp_place = lax.axis_index("tp")
    me = lax.axis_index("req")
    experts = lax.axis_size("req")
    attended = attend(fresh_qkv, kv_cache, cache_len)
    partial_value = jnp.dot(attended, out_proj, preferred_element_type=jnp.float32)
    summed = lax.psum(partial_value, "tp")
    hidden = (residual.astype(jnp.float32) + summed).astype(jnp.bfloat16)
    normed = rms_normed(hidden, norm_gain)
    rows = lax.all_gather(normed, "req", axis=0, tiled=True)
    logits = jnp.dot(normed.astype(jnp.float32), router_weight, precision=lax.Precision.HIGHEST)
    named = jnp.any(
        expert_ids[:, :, None] == jnp.arange(experts, dtype=jnp.int32)[None, None, :], axis=1
    )
    gates = jax.nn.softmax(jnp.where(named, logits, -jnp.inf), axis=-1)
    gates_all = lax.all_gather(gates, "req", axis=0, tiled=True)
    mine = jnp.arange(experts, dtype=jnp.int32)[None, :] == me
    weight = jnp.sum(jnp.where(mine, gates_all, 0.0), axis=1, keepdims=True)
    gate_part = jnp.dot(rows, gate_up[0, :, 0], preferred_element_type=jnp.float32)
    up_part = jnp.dot(rows, gate_up[0, :, 1], preferred_element_type=jnp.float32)
    inner = (jax.nn.silu(gate_part) * up_part).astype(jnp.bfloat16)
    result = jnp.dot(inner, down_proj[0], preferred_element_type=jnp.float32)
    own = lax.psum_scatter(result * weight, "tp", scatter_dimension=1, tiled=True)
    moe_share = lax.psum_scatter(own, "req", scatter_dimension=0, tiled=True)
    width_here = moe_share.shape[1]
    own_cols = lax.dynamic_slice_in_dim(hidden, tp_place * width_here, width_here, 1)
    return (own_cols.astype(jnp.float32) + moe_share).astype(jnp.bfloat16)


def solution(mesh):
    in_specs = (
        P("req", None),
        P("req", None, "tp"),
        P("req", None, None, "tp"),
        P("req"),
        P("tp", None),
        P(),
        P(),
        P("req", None),
        P("req", None, None, "tp"),
        P("req", "tp", None),
    )
    out_specs = P("req", "tp")
    return jax.shard_map(local, mesh=mesh, in_specs=in_specs, out_specs=out_specs, check_vma=False)
```

profile of v0, /device:TPU:0, one launch (start us, length us, event | category | flops | bytes accessed | tf_op | source)
XLA Modules:
  0.0 234.0 jit_solution(13227113264910571109)
XLA Ops:
  6.5 0.8 iota_compare_fusion.1
  7.4 0.9 convert_bitcast_fusion
  8.4 0.1 fusion.20
  8.5 0.1 copy.30
  8.5 0.1 reshape.54
  8.6 17.1 %slice_reduce_fusion = (bf16[32,24,1024]{2,1,0:T(8,128)(2,1)}, bf16[32,24,1024]{2,1,0:T(8,128)(2,1)S(1)}) fusion(bf16[32,24,2,1024]{3,2,1,0:T(2,128)(2,1)} %param.12), kind=kLoop, calls=%fused_computation.1 | loop fusion | bytes 6291456 | tf_op jit(solution)/shard_map/slice | solution.py:22
  25.7 0.9 fusion.6
  26.7 0.1 copy.26
  26.9 0.1 copy.20
  27.0 0.2 copy.31
  27.2 2.0 fusion.3
  29.2 0.1 fusion.19
  29.3 3.8 %fusion.24 = f32[32,2048]{1,0:T(8,128)} fusion(bf16[1024,2048]{1,0:T(8,128)(2,1)} %param.14, bf16[4,8,8,128]{3,2,1,0:T(8,128)(2,1)S(1)} %bitcast.84), kind=kOutput, calls=%fused_computation.40 | convolution fusion | flops 134217728 | bytes 4521984 | tf_op jit(solution)/shard_map/dot_general | solution.py:60
  33.1 0.0 all-reduce.2.cloned.1.call-update
  33.1 0.0 all-gather.3.cloned.1.call-start
  33.2 21.1 %all-reduce.2.cloned.1.call-done = f32[32,2048]{1,0:T(8,128)} async-done(((f32[32,2048]{1,0:T(8,128)}), f32[32,2048]{1,0:T(8,128)}) %all-reduce.2.cloned.1.call-update) | async-done | bytes 262160 | tf_op jit(solution)/shard_map/psum | solution.py:61
  54.3 1.1 fusion.15
  55.4 0.7 fusion.17
  56.1 0.0 all-gather.3.cloned.1.call-update
  56.1 0.0 reduce-scatter.3.cloned.1.call-start
  56.3 10.4 %fusion.33 = (bf16[1,2048,1,512]{3,2,1,0:T(2,128)(2,1)}, bf16[1,2048,1,512]{3,2,1,0:T(2,128)(2,1)}) fusion(bf16[1,2048,2,512]{3,2,1,0:T(2,128)(2,1)} %param.18), kind=kLoop, calls=%fused_computation.61 | loop fusion | bytes 8388608 | tf_op jit(solution)/shard_map/slice | solution.py:73
  66.7 0.2 fusion.34
  67.0 41.8 %all-gather = f32[16,32,16]{1,2,0:T(8,128)S(1)} all-gather(f32[1,32,16]{1,2,0:T(8,128)S(1)} %divide_bitcast_fusion), channel_id=1, replica_groups=mesh['req'=16,'tp'=2] {'req'}, dimensions={0}, use_global_device_ids=true | all-gather | bytes 34816 | tf_op jit(solution)/shard_map/all_gather | solution.py:70
  108.9 0.1 reshape.46
  109.0 0.1 select_reduce_fusion
  109.1 10.6 %all-gather.3.cloned.1.call-done = bf16[512,2048]{1,0:T(8,128)(2,1)} async-done(((bf16[32,2048]{1,0:T(8,128)(2,1)}), bf16[512,2048]{1,0:T(8,128)(2,1)}) %all-gather.3.cloned.1.call-update) | async-done | bytes 2097168 | tf_op jit(solution)/shard_map/all_gather | solution.py:64
  119.6 4.1 %fusion.1 = f32[512,512]{1,0:T(8,128)S(1)} fusion(bf16[512,2048]{1,0:T(8,128)(2,1)} %all-gather.3.cloned.1.call-done, bf16[1,2048,1,512]{3,2,1,0:T(2,128)(2,1)} %get-tuple-element.9), kind=kOutput, calls=%fused_computation.6 | convolution fusion | flops 1073741824 | bytes 5242880 | tf_op jit(solution)/shard_map/dot_general | solution.py:73
  123.7 7.3 %convolution_multiply_fusion = f32[512,2048]{1,0:T(8,128)} fusion(bf16[1,512,2048]{2,1,0:T(8,128)(2,1)S(1)} %copy-done, f32[512]{0:T(512)S(1)} %select_reduce_fusion, bf16[512,2048]{1,0:T(8,128)(2,1)} %all-gather.3.cloned.1.call-done, bf16[1,2048,1,512]{3,2,1,0:T(2,128)(2,1)} %get-tuple-element.10, f32[512,512]{1,0:T(8,128)S(1)} %fusion.1), kind=kOutput, calls=%fused_computation | convolution fusion | flops 2150105088 | bytes 11536384 | tf_op jit(solution)/shard_map/dot_general | solution.py:76
  131.0 0.0 reduce-scatter.5.cloned.1.call-start
  131.1 10.8 %reduce-scatter.3.cloned.1.call-done = f32[512,1024]{1,0:T(8,128)} async-done(((f32[512,2048]{1,0:T(8,128)}), f32[512,1024]{1,0:T(8,128)}) %reduce-scatter.3.cloned.1.call-update) | async-done | bytes 2097168 | tf_op jit(solution)/shard_map/reduce_scatter | solution.py:77
  141.9 84.1 %reduce-scatter.5.cloned.1.call-done = f32[32,1024]{1,0:T(8,128)} async-done(((f32[512,1024]{1,0:T(8,128)}), f32[32,1024]{1,0:T(8,128)}) %reduce-scatter.5.cloned.1.call-update) | async-done | bytes 131088 | tf_op jit(solution)/shard_map/reduce_scatter | solution.py:78
  226.0 1.5 add_convert_fusion.1
  (29 shorter events, 0.4 us)
Async XLA Ops:
  6.5 117.2 %copy-start = (bf16[1,512,2048]{2,1,0:T(8,128)(2,1)S(1)}, bf16[1,512,2048]{2,1,0:T(8,128)(2,1)}, u32[]{:S(2)}) copy-start(bf16[1,512,2048]{2,1,0:T(8,128)(2,1)} %param.19) | copy-start | bytes 6291460
  6.5 47.7 %all-reduce.2.cloned.1.call-start = ((), (), s32[]{:S(2)}) async-start(), calls=%async_computation.2 | async-start | bytes 524288 | tf_op jit(solution)/shard_map/psum | solution.py:61
  29.3 25.0 %copy-start.2 = (bf16[32,2048]{1,0:T(8,128)(2,1)S(1)}, bf16[32,2048]{1,0:T(8,128)(2,1)}, u32[]{:S(2)}) copy-start(bf16[32,2048]{1,0:T(8,128)(2,1)} %param.10) | copy-start | bytes 393220
  29.3 26.1 %copy-start.4 = (f32[2048]{0:T(1024)S(1)}, f32[2048]{0:T(1024)}, u32[]{:S(2)}) copy-start(f32[2048]{0:T(1024)} %param.15) | copy-start | bytes 24580
  29.3 26.9 %copy-start.5 = (s32[32,8]{0,1:T(8,128)S(1)}, s32[32,8]{0,1:T(8,128)}, u32[]{:S(2)}) copy-start(s32[32,8]{0,1:T(8,128)} %param.17) | copy-start | bytes 3076
  33.1 86.5 %all-gather.3.cloned.1.call-start = ((), (), s32[]{:S(2)}) async-start(), calls=%async_computation.3 | async-start | bytes 2228224 | tf_op jit(solution)/shard_map/all_gather | solution.py:64
  56.1 85.7 %reduce-scatter.3.cloned.1.call-start = ((), (), s32[]{:S(2)}) async-start(), calls=%async_computation.4 | async-start | bytes 6291456 | tf_op jit(solution)/shard_map/reduce_scatter | solution.py:77
  56.2 10.5 %copy-start.1 = (bf16[32,2048]{1,0:T(8,128)(2,1)S(1)}, bf16[32,2048]{1,0:T(8,128)(2,1)}, u32[]{:S(2)}) copy-start(bf16[32,2048]{1,0:T(8,128)(2,1)} %fusion.17) | copy-start | bytes 393220
  56.3 10.5 %copy-start.3 = (f32[2048,16]{0,1:T(8,128)S(1)}, f32[2048,16]{0,1:T(8,128)}, u32[]{:S(2)}) copy-start(f32[2048,16]{0,1:T(8,128)} %param.16) | copy-start | bytes 393220
  131.0 95.0 %reduce-scatter.5.cloned.1.call-start = ((), (), s32[]{:S(2)}) async-start(), calls=%async_computation.5 | async-start | bytes 2228224 | tf_op jit(solution)/shard_map/reduce_scatter | solution.py:78
Sparse Core Ops, SparseCore 0:
  33.3 20.9 all-reduce.1
  57.4 62.1 all-gather.2
  131.1 10.6 reduce-scatter.2
  144.0 81.9 reduce-scatter.4
where the time goes:
time: 234 us
  waiting for transfers between devices  127 us (54%)
  blocking collectives  41.8 us (18%)
  local copies, waits for them, and re-layouts  28.3 us (12%)
  matrix products  18.2 us (8%)
  between operations  13.3 us (6%)
  other arithmetic  5.64 us (2%)
    reduce_scatter x1, waiting for transfers between devices, local(): moe_share = lax.psum_scatter(own, 'req', scatter_dimension=0, tiled=True)  84.1 us
    all_gather x1, blocking collectives, local(): gates_all = lax.all_gather(gates, 'req', axis=0, tiled=True)  41.8 us
    psum x1, waiting for transfers between devices, local(): summed = lax.psum(partial_value, 'tp')  21.1 us
    slice x1, local copies, waits for them, and re-layouts, attend(): cache_values = kv_cache[:, :, 1].reshape(requests, ctx_len, local_heads, HD)  17.1 us
    reduce_scatter x1, waiting for transfers between devices, local(): lax.psum_scatter(result * weight, 'tp', scatter_dimension=1, tiled=True)  10.8 us
    all_gather x1, waiting for transfers between devices, local(): rows = lax.all_gather(normed, 'req', axis=0, tiled=True)  10.6 us
    slice x1, local copies, waits for them, and re-layouts, local(): gate_up[0, :, 0]  10.4 us
    dot_general x1, matrix products, local(): result = jnp.dot(inner, down_proj[0], preferred_element_type=jnp.float32)  7.25 us
  transfers between devices with their start and end apart: 4, of which 4 were waited for; matrix products, arithmetic and copies ran while one was open for 5% of the time, Pallas kernels for 0%

commit v1 on v0

--- a/solution.py
+++ b/solution.py
@@ -61,7 +61,14 @@
     summed = lax.psum(partial_value, "tp")
     hidden = (residual.astype(jnp.float32) + summed).astype(jnp.bfloat16)
     normed = rms_normed(hidden, norm_gain)
-    rows = lax.all_gather(normed, "req", axis=0, tiled=True)
+    ways, here = (lax.axis_size("req"), lax.axis_index("req"))
+    rows, reach = (normed, 1)
+    while reach < ways:
+        theirs = lax.ppermute(rows, "req", [(d, d ^ reach) for d in range(ways)])
+        mine_first = jnp.concatenate([rows, theirs], axis=0)
+        theirs_first = jnp.concatenate([theirs, rows], axis=0)
+        rows = jnp.where(here & reach == 0, mine_first, theirs_first)
+        reach = 2 * reach
     logits = jnp.dot(normed.astype(jnp.float32), router_weight, precision=lax.Precision.HIGHEST)
     named = jnp.any(
         expert_ids[:, :, None] == jnp.arange(experts, dtype=jnp.int32)[None, None, :], axis=1

time: 234 us -> 275 us (1.18)
  waiting for transfers between devices: 127 us -> 144 us
  blocking collectives: 41.8 us -> 51.5 us
  starting transfers between devices: 0.13 us -> 8.17 us
  matrix products: 18.2 us -> 21.1 us
    ppermute x0 -> x4, waiting for transfers between devices: none -> 20.7 us  [local(): theirs = lax.ppermute(rows, 'req', [(d, d ^ reach) for d in range(ways)])]
    all_gather x1 -> x0, waiting for transfers between devices: 10.6 us -> none  [local(): rows = lax.all_gather(normed, 'req', axis=0, tiled=True)]
    all_gather x1, blocking collectives: 41.8 us -> 51.5 us  [local(): gates_all = lax.all_gather(gates, 'req', axis=0, tiled=True)]
    ppermute x0 -> x4, starting transfers between devices: none -> 8.08 us  [local(): theirs = lax.ppermute(rows, 'req', [(d, d ^ reach) for d in range(ways)])]
    reduce_scatter x1, waiting for transfers between devices: 10.8 us -> 18.4 us  [local(): lax.psum_scatter(result * weight, 'tp', scatter_dimension=1, tiled=True)]
    select_n x0 -> x3, other arithmetic: none -> 2.78 us  [local(): rows = jnp.where(here & reach == 0, mine_first, theirs_first)]
  transfers between devices with their start and end apart: 4 -> 7, of which waited for: 4 -> 6; matrix products, arithmetic and copies ran while one was open for 5% -> 4% of each run, Pallas kernels for 0% -> 0%
where the time goes in v1:
time: 275 us; the launch traced here: 274 us
  waiting for transfers between devices  144 us (52%)
  blocking collectives  51.5 us (19%)
  local copies, waits for them, and re-layouts  28.2 us (10%)
  matrix products  21.1 us (8%)
  between operations  13.3 us (5%)
  starting transfers between devices  8.17 us (3%)
  other arithmetic  7.77 us (3%)
    reduce_scatter x1, waiting for transfers between devices, local(): moe_share = lax.psum_scatter(own, 'req', scatter_dimension=0, tiled=True)  84.1 us
    all_gather x1, blocking collectives, local(): gates_all = lax.all_gather(gates, 'req', axis=0, tiled=True)  51.5 us
    psum x1, waiting for transfers between devices, local(): summed = lax.psum(partial_value, 'tp')  21.1 us
    ppermute x4, waiting for transfers between devices, local(): theirs = lax.ppermute(rows, 'req', [(d, d ^ reach) for d in range(ways)])  20.7 us
    reduce_scatter x1, waiting for transfers between devices, local(): lax.psum_scatter(result * weight, 'tp', scatter_dimension=1, tiled=True)  18.4 us
    slice x1, local copies, waits for them, and re-layouts, attend(): cache_values = kv_cache[:, :, 1].reshape(requests, ctx_len, local_heads, HD)  17.1 us
    slice x1, local copies, waits for them, and re-layouts, local(): gate_up[0, :, 0]  10.4 us
    dot_general x1, matrix products, local(): result = jnp.dot(inner, down_proj[0], preferred_element_type=jnp.float32)  8.36 us
  transfers between devices with their start and end apart: 7, of which 6 were waited for; matrix products, arithmetic and copies ran while one was open for 4% of the time, Pallas kernels for 0%

profile of v1, /device:TPU:0, one launch (start us, length us, event | category | flops | bytes accessed | tf_op | source)
XLA Modules:
  0.0 274.5 jit_solution(7646172629015376529)
XLA Ops:
  6.5 0.8 iota_compare_fusion.1
  7.4 0.9 convert_bitcast_fusion
  8.4 0.1 fusion.15
  8.6 17.1 %slice_reduce_fusion = (bf16[32,24,1024]{2,1,0:T(8,128)(2,1)}, bf16[32,24,1024]{2,1,0:T(8,128)(2,1)S(1)}) fusion(bf16[32,24,2,1024]{3,2,1,0:T(2,128)(2,1)} %param.12), kind=kLoop, calls=%fused_computation.1 | loop fusion | bytes 6291456 | tf_op jit(solution)/shard_map/slice | solution.py:22
  25.7 0.9 fusion.6
  26.7 0.1 copy.26
  27.0 0.2 copy.31
  27.2 2.0 fusion.3
  29.2 0.1 fusion.14
  29.3 3.8 %fusion.19 = f32[32,2048]{1,0:T(8,128)} fusion(bf16[1024,2048]{1,0:T(8,128)(2,1)} %param.14, bf16[4,8,8,128]{3,2,1,0:T(8,128)(2,1)S(1)} %bitcast.80), kind=kOutput, calls=%fused_computation.40 | convolution fusion | flops 134217728 | bytes 4521984 | tf_op jit(solution)/shard_map/dot_general | solution.py:60
  33.1 21.1 %all-reduce.2.cloned.1.call-done = f32[32,2048]{1,0:T(8,128)} async-done(((f32[32,2048]{1,0:T(8,128)}), f32[32,2048]{1,0:T(8,128)}) %all-reduce.2.cloned.1.call-update) | async-done | bytes 262160 | tf_op jit(solution)/shard_map/psum | solution.py:61
  54.2 1.1 fusion.10
  55.3 0.1 fusion.12
  55.4 1.8 collective-permute-start
  57.2 4.0 %collective-permute-done = bf16[32,2048]{1,0:T(8,128)(2,1)S(1)} collective-permute-done((bf16[32,2048]{1,0:T(8,128)(2,1)S(1)}, bf16[32,2048]{1,0:T(8,128)(2,1)S(1)}, u32[]{:S(2)}, u32[]{:S(2)}) %collective-permute-start) | collective-permute-done | bytes 131104 | tf_op jit(solution)/shard_map/ppermute | solution.py:67
  61.2 1.8 collective-permute-start.1
  63.1 6.0 %collective-permute-done.1 = bf16[64,2048]{1,0:T(8,128)(2,1)S(1)} collective-permute-done((bf16[64,2048]{1,0:T(8,128)(2,1)S(1)}, bf16[64,2048]{1,0:T(8,128)(2,1)S(1)}, u32[]{:S(2)}, u32[]{:S(2)}) %collective-permute-start.1) | collective-permute-done | bytes 262176 | tf_op jit(solution)/shard_map/ppermute | solution.py:67
  69.0 0.1 maximum_select_fusion.2
  69.1 1.8 collective-permute-start.2
  70.9 10.8 %collective-permute-done.2 = bf16[128,2048]{1,0:T(8,128)(2,1)} collective-permute-done((bf16[128,2048]{1,0:T(8,128)(2,1)S(1)}, bf16[128,2048]{1,0:T(8,128)(2,1)}, u32[]{:S(2)}, u32[]{:S(2)}) %collective-permute-start.2) | collective-permute-done | bytes 524320 | tf_op jit(solution)/shard_map/ppermute | solution.py:67
  81.7 2.6 maximum_select_fusion.1
  84.3 2.7 collective-permute-start.3
  87.0 10.4 %fusion.31 = (bf16[1,2048,1,512]{3,2,1,0:T(2,128)(2,1)}, bf16[1,2048,1,512]{3,2,1,0:T(2,128)(2,1)}) fusion(bf16[1,2048,2,512]{3,2,1,0:T(2,128)(2,1)} %param.18), kind=kLoop, calls=%fused_computation.63 | loop fusion | bytes 8388608 | tf_op jit(solution)/shard_map/slice | solution.py:80
  97.5 0.2 fusion.32
  97.7 51.5 %all-gather = f32[16,32,16]{1,2,0:T(8,128)S(1)} all-gather(f32[1,32,16]{1,2,0:T(8,128)S(1)} %divide_bitcast_fusion), channel_id=1, replica_groups=mesh['req'=16,'tp'=2] {'req'}, dimensions={0}, use_global_device_ids=true | all-gather | bytes 34816 | tf_op jit(solution)/shard_map/all_gather | solution.py:77
  149.3 0.1 reshape.46
  149.4 0.1 select_reduce_fusion
  149.5 5.9 %fusion = f32[512,512]{1,0:T(8,128)} fusion(bf16[1,2048,1,512]{3,2,1,0:T(2,128)(2,1)} %get-tuple-element.10, bf16[256,2048]{1,0:T(8,128)(2,1)} %collective-permute-done.3, bf16[256,2048]{1,0:T(8,128)(2,1)} %maximum_select_fusion.1, pred[]{:T(512)S(6)} %eq.36), kind=kOutput, calls=%fused_computation.5 | convolution fusion | flops 1083179008 | bytes 5242881 | tf_op jit(solution)/shard_map/dot_general | solution.py:81
  155.4 8.4 %convolution_multiply_fusion = f32[512,2048]{1,0:T(8,128)} fusion(bf16[1,512,2048]{2,1,0:T(8,128)(2,1)S(1)} %copy-done, f32[512]{0:T(512)S(1)} %select_reduce_fusion, f32[512,512]{1,0:T(8,128)} %fusion, bf16[1,2048,1,512]{3,2,1,0:T(2,128)(2,1)} %get-tuple-element.9, bf16[256,2048]{1,0:T(8,128)(2,1)} %collective-permute-done.3, ...), kind=kOutput, calls=%fused_computation | convolution fusion | flops 2159542272 | bytes 11536385 | tf_op jit(solution)/shard_map/dot_general | solution.py:83
  163.8 18.4 %reduce-scatter.3.cloned.1.call-done = f32[512,1024]{1,0:T(8,128)} async-done(((f32[512,2048]{1,0:T(8,128)}), f32[512,1024]{1,0:T(8,128)}) %reduce-scatter.3.cloned.1.call-update) | async-done | bytes 2097168 | tf_op jit(solution)/shard_map/reduce_scatter | solution.py:84
  182.3 84.1 %reduce-scatter.5.cloned.1.call-done = f32[32,1024]{1,0:T(8,128)} async-done(((f32[512,1024]{1,0:T(8,128)}), f32[32,1024]{1,0:T(8,128)}) %reduce-scatter.5.cloned.1.call-update) | async-done | bytes 131088 | tf_op jit(solution)/shard_map/reduce_scatter | solution.py:85
  266.4 1.5 add_convert_fusion.1
  (35 shorter events, 0.7 us)
Async XLA Ops:
  6.5 148.8 %copy-start = (bf16[1,512,2048]{2,1,0:T(8,128)(2,1)S(1)}, bf16[1,512,2048]{2,1,0:T(8,128)(2,1)}, u32[]{:S(2)}) copy-start(bf16[1,512,2048]{2,1,0:T(8,128)(2,1)} %param.19) | copy-start | bytes 6291460
  6.5 47.7 %all-reduce.2.cloned.1.call-start = ((), (), s32[]{:S(2)}) async-start(), calls=%async_computation.2 | async-start | bytes 524288 | tf_op jit(solution)/shard_map/psum | solution.py:61
  29.3 24.9 %copy-start.1 = (bf16[32,2048]{1,0:T(8,128)(2,1)S(1)}, bf16[32,2048]{1,0:T(8,128)(2,1)}, u32[]{:S(2)}) copy-start(bf16[32,2048]{1,0:T(8,128)(2,1)} %param.10) | copy-start | bytes 393220
  29.3 26.0 %copy-start.3 = (f32[2048]{0:T(1024)S(1)}, f32[2048]{0:T(1024)}, u32[]{:S(2)}) copy-start(f32[2048]{0:T(1024)} %param.15) | copy-start | bytes 24580
  33.1 149.1 %reduce-scatter.3.cloned.1.call-start = ((), (), s32[]{:S(2)}) async-start(), calls=%async_computation.3 | async-start | bytes 6291456 | tf_op jit(solution)/shard_map/reduce_scatter | solution.py:84
  55.4 5.8 %collective-permute-start = (bf16[32,2048]{1,0:T(8,128)(2,1)S(1)}, bf16[32,2048]{1,0:T(8,128)(2,1)S(1)}, u32[]{:S(2)}, u32[]{:S(2)}) collective-permute-start(bf16[32,2048]{1,0:T(8,128)(2,1)S(1)} %fusion.12), channel_id=1, source_target_pairs={{0,2},{2,0},{4,6},{6,4},{8,10},{10,8},{12,14},{14,12},{16,18},{18,... | collective-permute-start | bytes 393224 | tf_op jit(solution)/shard_map/ppermute | solution.py:67
  61.2 7.8 %collective-permute-start.1 = (bf16[64,2048]{1,0:T(8,128)(2,1)S(1)}, bf16[64,2048]{1,0:T(8,128)(2,1)S(1)}, u32[]{:S(2)}, u32[]{:S(2)}) collective-permute-start(bf16[64,2048]{1,0:T(8,128)(2,1)S(1)} %maximum_select_fusion.6), channel_id=1, source_target_pairs={{0,4},{2,6},{4,0},{6,2},{8,12},{10,14},{12,8},{14,10},{16,20},{18,... | collective-permute-start | bytes 786440 | tf_op jit(solution)/shard_map/ppermute | solution.py:67
  69.1 12.6 %collective-permute-start.2 = (bf16[128,2048]{1,0:T(8,128)(2,1)S(1)}, bf16[128,2048]{1,0:T(8,128)(2,1)}, u32[]{:S(2)}, u32[]{:S(2)}) collective-permute-start(bf16[128,2048]{1,0:T(8,128)(2,1)S(1)} %maximum_select_fusion.2), channel_id=1, source_target_pairs={{0,8},{2,10},{4,12},{6,14},{8,0},{10,2},{12,4},{14,6},{16,24},{18,... | collective-permute-start | bytes 1572872 | tf_op jit(solution)/shard_map/ppermute | solution.py:67
  84.3 13.1 %copy-start.4 = (s32[32,8]{0,1:T(8,128)S(1)}, s32[32,8]{0,1:T(8,128)}, u32[]{:S(2)}) copy-start(s32[32,8]{0,1:T(8,128)} %param.17) | copy-start | bytes 3076
  84.3 13.1 %copy-start.2 = (f32[2048,16]{0,1:T(8,128)S(1)}, f32[2048,16]{0,1:T(8,128)}, u32[]{:S(2)}) copy-start(f32[2048,16]{0,1:T(8,128)} %param.16) | copy-start | bytes 393220
  84.3 65.1 %collective-permute-start.3 = (bf16[256,2048]{1,0:T(8,128)(2,1)}, bf16[256,2048]{1,0:T(8,128)(2,1)}, u32[]{:S(2)}, u32[]{:S(2)}) collective-permute-start(bf16[256,2048]{1,0:T(8,128)(2,1)} %maximum_select_fusion.1), channel_id=1, source_target_pairs={{0,16},{2,18},{4,20},{6,22},{8,24},{10,26},{12,28},{14,30},{16,0},... | collective-permute-start | bytes 3145736 | tf_op jit(solution)/shard_map/ppermute | solution.py:67
  163.7 102.7 %reduce-scatter.5.cloned.1.call-start = ((), (), s32[]{:S(2)}) async-start(), calls=%async_computation.4 | async-start | bytes 2228224 | tf_op jit(solution)/shard_map/reduce_scatter | solution.py:85
Sparse Core Ops, SparseCore 0:
  33.2 20.9 all-reduce.1
  163.9 18.3 reduce-scatter.2
  184.5 81.8 reduce-scatter.4
